TPU v7x, 512 devices: a whole 4x8x8 slice. The times are simulated.
512 devices in a mesh: param: 32 (over x, y), ex: 16 (over z, core).
Axes of the slice: x: 4, y: 8, z: 8, core: 2. Of those that a mesh axis runs over, the one named last changes fastest.
Arguments:
- act_factor: bfloat16 [16384, 4096], P('ex', 'param'), may hold values from -6 to 6
- grad_factor: bfloat16 [16384, 4096], P('ex', 'param'), may hold values from -6 to 6
- proj_bank: bfloat16 [16, 128, 128], replicated, may hold values from -0.5 to 0.5
- tile_rows: int32 [256], replicated, may hold values from 0 to 31
- tile_cols: int32 [256], replicated, may hold values from 0 to 31
- tile_out: int32 [256], replicated, may hold values from 0 to 7
- bank_left: int32 [256], replicated, may hold values from 0 to 15
- bank_right: int32 [256], replicated, may hold values from 0 to 15
- owner_map: int32 [16, 32], P('ex'), may hold values from 0 to 31, each once within a row
Outputs:
- features: float32 [512, 1024], P(('ex', 'param'))
- factor_r: float32 [1024, 1024], P('param', 'ex')
Inputs may be any that keep to these rules, and one draw needn't show every extreme that they name: Each row of owner_map is a permutation of the 32 examples of its group.
All inputs are finite; a program needn't handle non-finite values.
Results may differ from a plain program's by a relative error of at most 0.0003.
Values may be sent and summed in bfloat16 or wider, within the bound.
No kernel may reach another device: no remote copies, remote signals or barrier semaphores. Data moves between devices by JAX's collectives and lax.ppermute only.
A program may use at most 64 MiB of HBM per device.

v0:
```python
import functools
import math

import jax
import jax.numpy as jnp
from jax import lax
from jax.experimental import pallas as pl
from jax.experimental.pallas import tpu as pltpu
from jax.sharding import PartitionSpec as P

TILE = 128
SUB = 8
DAMPING = 0.25
PIECES = 3
AHEAD = 4
LEVELS = 32767.0
STEPS = 16.0
f32, bf16 = jnp.float32, jnp.bfloat16


def project_kernel(
    seq_len, scale, rows_ref, cols_ref, outs_ref, lefts_ref, rights_ref, x_ref, bank_ref, feat_ref, table, acc
):
    banks = bank_ref.shape[0]
    for pair in range(banks // 2):
        tiles = jnp.concatenate([bank_ref[2 * pair], bank_ref[2 * pair + 1]], axis=1)
        both = jnp.dot(x_ref[...], tiles, preferred_element_type=f32)
        table[2 * pair] = both[:, :TILE]
        table[2 * pair + 1] = both[:, TILE:]
    acc[...] = jnp.zeros_like(acc)
    unroll = 8

    def add_slots(group, carry):
        for k in range(unroll):
            s = group * unroll + k
            left_at = pl.multiple_of(rows_ref[s] * (2 * seq_len), seq_len)
            right_at = pl.multiple_of(cols_ref[s] * (2 * seq_len) + seq_len, seq_len)
            left = table[lefts_ref[s], pl.ds(left_at, seq_len), :]
            right = table[rights_ref[s], pl.ds(right_at, seq_len), :]
            term = jnp.sum((left * right).reshape(seq_len // SUB, SUB, TILE), axis=0)
            acc[outs_ref[s]] += term
        return carry

    lax.fori_loop(0, rows_ref.shape[0] // unroll, add_slots, 0)
    feat_ref[...] = jnp.sum(acc[...], axis=1) * scale


def project(x, bank, ids, seq_len, out_tiles):
    scale = 1.0 / math.sqrt(seq_len * ids[0].shape[0] / out_tiles)
    smem = pl.BlockSpec(memory_space=pltpu.SMEM)
    vmem = pl.BlockSpec(memory_space=pltpu.VMEM)
    return pl.pallas_call(
        functools.partial(project_kernel, seq_len, scale),
        out_shape=jax.ShapeDtypeStruct((out_tiles, TILE), f32),
        in_specs=[smem] * 5 + [vmem] * 2,
        out_specs=vmem,
        scratch_shapes=[
            pltpu.VMEM((bank.shape[0], x.shape[0], TILE), f32),
            pltpu.VMEM((out_tiles, SUB, TILE), f32),
        ],
        compiler_params=pltpu.CompilerParams(vmem_limit_bytes=40 * 2**20),
        name="project",
    )(*ids, x, bank)


def factor_block(rows):
    groups = len(rows)
    lane = lax.broadcasted_iota(jnp.int32, (SUB, TILE), 1)
    sub = lax.broadcasted_iota(jnp.int32, (SUB, TILE), 0)
    rows = list(rows)

    def column(p, c):
        return jnp.broadcast_to(rows[p][:, c : c + 1], (SUB, TILE))

    def entry(x, s):
        return jnp.broadcast_to(x[s : s + 1, :], (SUB, TILE))

    def wanted(i, first):
        for c in range(max(i, 0), min(TILE, i + SUB + 1)):
            for p in range(first, groups):
                if c <= i + AHEAD or p <= c // SUB:
                    yield c, p

    spread = {(c, p): column(p, c) for c, p in wanted(-1, 0)}
    small, upper, inverse_lower = {}, [], []
    for i in range(TILE):
        q, s = divmod(i, SUB)
        if s == 0:
            small = {(k, l): entry(spread[SUB * q + l, q], k) for k in range(SUB) for l in range(k, SUB)}
            root = None
        inverse = 1.0 / small[s, s]
        one_root = lax.rsqrt(small[s, s])
        root = one_root if root is None else jnp.where(sub == s, one_root, root)
        weights = {SUB * q + l: small[s, l] * inverse for l in range(s + 1, SUB)}
        for l in range(s + 1, SUB):
            for m in range(l, SUB):
                small[l, m] = small[l, m] - small[s, m] * weights[SUB * q + l]
        at_pivot, below = lane == i, sub > s
        row = jnp.where(at_pivot, 1.0, entry(rows[q], s)) * inverse
        own = jnp.where(below, spread[i, q], 0.0)
        for c in sorted({c for c, _ in spread if c > i}):
            if c not in weights:
                weights[c] = entry(spread[c, q], s) * inverse
            for p in range(q, groups):
                if (c, p) in spread:
                    spread[c, p] = spread[c, p] - (own if p == q else spread[i, p]) * weights[c]
        if s < SUB - 1:
            rows[q] = jnp.where(at_pivot & below, 0.0, rows[q]) - own * row
        for p in range(q + 1, groups):
            rows[p] = jnp.where(at_pivot, 0.0, rows[p]) - spread[i, p] * row
        if s == SUB - 1:
            r = sub + SUB * q
            upper.append(jnp.where(lane >= r, rows[q], 0.0) * root)
            inverse_lower.append(jnp.where(lane < r, rows[q], jnp.where(lane == r, 1.0, 0.0)) * root)
        first = (i + 1) // SUB
        spread = {(c, p): v for (c, p), v in spread.items() if c > i and p >= first}
        for c, p in wanted(i, first):
            if c > i and (c, p) not in spread:
                spread[c, p] = column(p, c)
    return jnp.concatenate(upper, 0), jnp.concatenate(inverse_lower, 0)


def split(x):
    pieces = []
    for k in range(PIECES):
        piece = x.astype(bf16)
        pieces.append(piece)
        if k < PIECES - 1:
            x = x - piece.astype(f32)
    return pieces


def times_t(a, b):
    total = None
    for i, k in sorted(((i, k) for i in range(PIECES) for k in range(PIECES) if i + k < max(PIECES, 3)), key=lambda ik: -sum(ik)):
        term = lax.dot_general(a[i], b[k], (((1,), (1,)), ((), ())), preferred_element_type=f32)
        total = term if total is None else total + term
    return total


def encode(rows):
    count, blocks, width = rows.shape
    top = jnp.max(jnp.abs(rows), axis=(1, 2), keepdims=True)
    step = jnp.ceil(STEPS * jnp.log2(jnp.maximum(top, 1e-30)))
    coded = jnp.clip(jnp.round(rows * (LEVELS * jnp.exp2(step / -STEPS))), -LEVELS, LEVELS)
    scales = jnp.broadcast_to(step[:, 0], (count, width))
    parts = [coded.reshape(count * blocks, width), scales, jnp.zeros((-count % 16, width), f32)]
    return jnp.concatenate(parts, axis=0).astype(jnp.int16)


def factor_kernel(place_ref, own_ref, other_ref, out_ref, lower, panels, feat, *pieces):
    ft, lp = pieces[:PIECES], pieces[PIECES:]
    examples, nb, _ = feat.shape
    peers = own_ref.shape[0]
    count = examples // (2 * peers)
    scale = 1.0 / examples
    for h, ref in enumerate((own_ref, other_ref)):

        def decode(peer, carry):
            coded = ref[peer].astype(jnp.int32).astype(f32)
            steps = coded[count * nb : count * nb + count]
            scales = jnp.exp2(steps * (1.0 / STEPS)) * (1.0 / LEVELS)
            values = coded[: count * nb].reshape(count, nb, TILE) * jnp.broadcast_to(scales[:, None, :], (count, nb, TILE))
            feat[pl.ds(h * peers * count + peer * count, count)] = values
            return carry

        lax.fori_loop(0, peers, decode, 0)
    for b in range(nb):
        for k, piece in enumerate(split(feat[:, b, :].T)):
            ft[k][b * TILE : (b + 1) * TILE, :] = piece

    def feats(lo, hi):
        return [ref[lo * TILE : hi * TILE, :] for ref in ft]

    def lows(lo, hi, to):
        return [ref[lo * TILE : hi * TILE, : to * TILE] for ref in lp]

    def put(lo, hi, c, value):
        lower[lo * TILE : hi * TILE, c * TILE : (c + 1) * TILE] = value
        for ref, piece in zip(lp, split(value)):
            ref[lo * TILE : hi * TILE, c * TILE : (c + 1) * TILE] = piece

    shape = (TILE, TILE)
    eye = lax.broadcasted_iota(jnp.int32, shape, 0) == lax.broadcasted_iota(jnp.int32, shape, 1)

    def diagonal(j, known):
        block = times_t(feats(j, j + 1), feats(j, j + 1)) * scale + jnp.where(eye, DAMPING, 0.0)
        if known:
            block = block - times_t(lows(j, j + 1, known), lows(j, j + 1, known))
        return block

    for i in range(nb):
        for c in range(i + 1, nb):
            lower[i * TILE : (i + 1) * TILE, c * TILE : (c + 1) * TILE] = jnp.zeros(shape, f32)

    block, inverse = diagonal(0, 0), None
    for j in range(nb):
        if j >= 1 and j + 1 < nb:
            put(j + 1, nb, j - 1, times_t(split(panels[(j - 1) % 2, (j + 1) * TILE :, :]), inverse))
        if j + 1 < nb:
            panel = times_t(feats(j + 1, nb), feats(j, j + 1)) * scale
            if j:
                panel = panel - times_t(lows(j + 1, nb, j), lows(j, j + 1, j))
            panels[j % 2, (j + 1) * TILE :, :] = panel
            ahead = diagonal(j + 1, j)
        upper, inverse = factor_block([block[SUB * q : SUB * (q + 1), :] for q in range(TILE // SUB)])
        lower[j * TILE : (j + 1) * TILE, j * TILE : (j + 1) * TILE] = upper.T
        if j + 1 < nb:
            inverse = split(inverse)
            first = times_t(split(panels[j % 2, (j + 1) * TILE : (j + 2) * TILE, :]), inverse)
            put(j + 1, j + 2, j, first)
            first = split(first)
            block = ahead - times_t(first, first)

    height, width = out_ref.shape
    ex, param = place_ref[0], place_ref[1]
    per_tile = TILE // height
    taken = lower[pl.ds(pl.multiple_of(ex * width, width), width), pl.ds(pl.multiple_of(param // per_tile * TILE, TILE), TILE)]
    flipped = taken.T
    result = flipped[:height]
    for k in range(1, per_tile):
        result = jnp.where(param % per_tile == k, flipped[k * height : (k + 1) * height], result)
    out_ref[...] = result


def factor(place, own, other, examples, nb, block_shape):
    width = nb * TILE
    vmem = pl.BlockSpec(memory_space=pltpu.VMEM)
    return pl.pallas_call(
        factor_kernel,
        out_shape=jax.ShapeDtypeStruct(block_shape, f32),
        in_specs=[pl.BlockSpec(memory_space=pltpu.SMEM), vmem, vmem],
        out_specs=vmem,
        scratch_shapes=[pltpu.VMEM((width, width), f32), pltpu.VMEM((2, width, TILE), f32), pltpu.VMEM((examples, nb, TILE), f32)]
        + [pltpu.VMEM((width, examples), bf16)] * PIECES
        + [pltpu.VMEM((width, width), bf16)] * PIECES,
        compiler_params=pltpu.CompilerParams(vmem_limit_bytes=48 * 2**20),
        name="factor",
    )(place, own, other)


def per_device(
    ex_size, act_factor, grad_factor, proj_bank, tile_rows, tile_cols, tile_out, bank_left, bank_right, owner_map
):
    group = owner_map.shape[1]
    tokens, width = act_factor.shape
    seq_len = tokens // group
    out_tiles = 1024 // width
    ex, param = lax.axis_index("ex"), lax.axis_index("param")

    both = jnp.concatenate([f.reshape(group, seq_len, width) for f in (act_factor, grad_factor)], axis=1)
    both = lax.all_to_all(both, "param", split_axis=0, concat_axis=0, tiled=True)
    feats = project(
        both.reshape(2 * tokens, width),
        proj_bank,
        (tile_rows, tile_cols, tile_out, bank_left, bank_right),
        seq_len,
        out_tiles,
    )

    chips = ex_size // 2
    lines = [[2 * z + core for z in range(chips)] for core in range(2)]
    line = lax.all_to_all(
        jnp.broadcast_to(feats[None], (chips,) + feats.shape),
        "ex",
        split_axis=0,
        concat_axis=0,
        axis_index_groups=lines,
        tiled=True,
    )
    coded = encode(line)
    own = lax.all_to_all(
        jnp.broadcast_to(coded[None], (group,) + coded.shape), "param", split_axis=0, concat_axis=0, tiled=True
    )
    other = lax.ppermute(own, "ex", [(i, i ^ 1) for i in range(ex_size)])

    mine, at = owner_map[0, param], ex // 2
    taken = lax.dynamic_slice(own, (mine, at * out_tiles, 0), (1, out_tiles, width)).astype(f32)
    step = lax.dynamic_slice(own, (mine, chips * out_tiles + at, 0), (1, 1, width)).astype(f32)
    features = (taken * (jnp.exp2(step / STEPS) / LEVELS)).reshape(1, out_tiles * width)
    block = (out_tiles * width // group, out_tiles * width // ex_size)
    place = jnp.stack([ex, param]).astype(jnp.int32)
    r_block = factor(place, own, other, group * ex_size, out_tiles, block)
    return features, r_block


def solution(mesh):
    placed = (P("ex", "param"), P("ex", "param"), P(), P(), P(), P(), P(), P(), P("ex", None))
    return jax.shard_map(
        functools.partial(per_device, mesh.shape["ex"]),
        mesh=mesh,
        in_specs=placed,
        out_specs=(P(("ex", "param"), None), P("param", "ex")),
        check_vma=False,
    )
```

profile of v0, /device:TPU:1, one launch (start us, length us, event | category | flops | bytes accessed | tf_op | source)
XLA Modules:
  0.0 120.2 jit_solution(656286488805087878)
XLA Ops:
  0.6 0.0 copy-start
  0.6 1.1 pad_maximum_fusion
  1.7 0.0 copy-start.1
  1.7 0.0 copy-start.3
  1.8 0.0 copy-start.4
  1.8 0.0 copy-start.5
  1.8 0.0 copy-start.6
  1.8 24.7 %all_to_all.15 = bf16[32,64,128]{2,1,0:T(8,128)(2,1)S(1)} all-to-all(bf16[32,64,128]{2,1,0:T(8,128)(2,1)S(1)} %pad_maximum_fusion), channel_id=1, replica_groups=mesh['param'=32,'ex'=16] {'param'}, dimensions={0} | all-to-all | bytes 1048576 | tf_op jit(solution)/shard_map/all_to_all | solution.py:252
  26.5 0.0 copy-start.2
  26.5 0.0 copy-done.1
  26.5 0.0 copy-done.3
  26.5 0.0 copy-done.4
  26.5 0.0 copy-done.5
  26.6 0.0 copy-done.6
  26.6 0.6 copy-done.2
  27.2 4.4 %project.1 = f32[8,128]{1,0:T(8,128)S(1)} custom-call(s32[256]{0:T(256)S(1)} %copy-done.2, s32[256]{0:T(256)S(1)} %copy-done.3, s32[256]{0:T(256)S(1)} %copy-done.4, s32[256]{0:T(256)S(1)} %copy-done.5, s32[256]{0:T(256)S(1)} %copy-done.6, bf16[2048,128]{1,0:T(8,128)(2,1)S(1)} %bitcast.11, bf16[16,128,128]{2,1,0:T(8,128)(2,1)S(1)} %copy-done.1), custom_call_target="tpu_custom_call" | custom-call | tf_op jit(solution)/shard_map/project/pallas_call | solution.py:52
  31.6 0.6 broadcast_in_dim.6
  32.2 10.0 %all-to-all-start.1 = ((f32[8,8,128]{2,1,0:T(8,128)}), f32[8,8,128]{2,1,0:T(8,128)S(1)}, u32[]{:S(2)}, u32[]{:S(2)}) async-start(f32[8,8,128]{2,1,0:T(8,128)} %broadcast_in_dim.6), calls=%async_computation.1 | async-start | bytes 65536 | tf_op jit(solution)/shard_map/all_to_all | solution.py:263
  42.2 0.1 pad.4.clone
  42.3 6.8 %all-to-all-done.1 = f32[8,8,128]{2,1,0:T(8,128)S(1)} async-done(((f32[8,8,128]{2,1,0:T(8,128)}), f32[8,8,128]{2,1,0:T(8,128)S(1)}, u32[]{:S(2)}, u32[]{:S(2)}) %all-to-all-start.1) | async-done | bytes 32800 | tf_op jit(solution)/shard_map/all_to_all | solution.py:263
  49.1 0.1 abs_reduce_fusion
  49.3 0.1 pad.3.clone
  49.4 0.1 fusion
  49.4 0.1 add_add_fusion
  49.5 0.1 broadcast_in_dim.8
  49.6 21.8 %all_to_all.16.own_ref = s16[32,80,128]{2,1,0:T(8,128)(2,1)S(1)} all-to-all(s16[32,80,128]{2,1,0:T(8,128)(2,1)S(1)} %broadcast_in_dim.8), channel_id=1, replica_groups=mesh['param'=32,'ex'=16] {'param'}, dimensions={0} | all-to-all | bytes 1310720 | tf_op jit(solution)/shard_map/all_to_all | solution.py:272
  71.5 8.3 %collective-permute-start = (s16[32,80,128]{2,1,0:T(8,128)(2,1)S(1)}, s16[32,80,128]{2,1,0:T(8,128)(2,1)S(1)}, u32[]{:S(2)}, u32[]{:S(2)}) collective-permute-start(s16[32,80,128]{2,1,0:T(8,128)(2,1)S(1)} %all_to_all.16.own_ref), channel_id=1, source_target_pairs={{0,1},{1,0},{2,3},{3,2},{4,5},{5,4},{6,7},{7,6},{8,9},{9,8},{10,11... | collective-permute-start | bytes 1966088 | tf_op jit(solution)/shard_map/ppermute | solution.py:275
  79.7 0.0 copy-done
  79.7 0.6 constant_dynamic-slice_fusion.1
  82.3 0.1 pad_add_fusion.place_ref
  82.4 0.6 convert_multiply_fusion
  83.0 0.0 collective-permute-done.other_ref
  83.0 37.2 %factor.1 = f32[32,64]{1,0:T(8,128)} custom-call(s32[2]{0:T(128)S(1)} %pad_add_fusion.place_ref, s16[32,80,128]{2,1,0:T(8,128)(2,1)S(1)} %all_to_all.16.own_ref, s16[32,80,128]{2,1,0:T(8,128)(2,1)S(1)} %collective-permute-done.other_ref), custom_call_target="tpu_custom_call" | custom-call | tf_op jit(solution)/shard_map/factor/pallas_call | solution.py:229
  (3 shorter events, 0.0 us)
Async XLA Ops:
  0.6 79.1 %copy-start = (s32[1,32]{1,0:T(1,128)S(1)}, s32[1,32]{1,0:T(1,128)}, u32[]{:S(2)}) copy-start(s32[1,32]{1,0:T(1,128)} %param.17) | copy-start | bytes 388
  1.7 24.8 %copy-start.1 = (bf16[16,128,128]{2,1,0:T(8,128)(2,1)S(1)}, bf16[16,128,128]{2,1,0:T(8,128)(2,1)}, u32[]{:S(2)}) copy-start(bf16[16,128,128]{2,1,0:T(8,128)(2,1)} %bank_ref.1) | copy-start | bytes 1572868
  1.7 24.8 %copy-start.3 = (s32[256]{0:T(256)S(1)}, s32[256]{0:T(256)}, u32[]{:S(2)}) copy-start(s32[256]{0:T(256)} %cols_ref.1) | copy-start | bytes 3076
  1.8 24.8 %copy-start.4 = (s32[256]{0:T(256)S(1)}, s32[256]{0:T(256)}, u32[]{:S(2)}) copy-start(s32[256]{0:T(256)} %outs_ref.1) | copy-start | bytes 3076
  1.8 24.8 %copy-start.5 = (s32[256]{0:T(256)S(1)}, s32[256]{0:T(256)}, u32[]{:S(2)}) copy-start(s32[256]{0:T(256)} %lefts_ref.1) | copy-start | bytes 3076
  1.8 24.8 %copy-start.6 = (s32[256]{0:T(256)S(1)}, s32[256]{0:T(256)}, u32[]{:S(2)}) copy-start(s32[256]{0:T(256)} %rights_ref.1) | copy-start | bytes 3076
  26.5 0.7 copy-start.2
  32.2 16.9 %all-to-all-start.1 = ((f32[8,8,128]{2,1,0:T(8,128)}), f32[8,8,128]{2,1,0:T(8,128)S(1)}, u32[]{:S(2)}, u32[]{:S(2)}) async-start(f32[8,8,128]{2,1,0:T(8,128)} %broadcast_in_dim.6), calls=%async_computation.1 | async-start | bytes 65536 | tf_op jit(solution)/shard_map/all_to_all | solution.py:263
  71.5 11.5 %collective-permute-start = (s16[32,80,128]{2,1,0:T(8,128)(2,1)S(1)}, s16[32,80,128]{2,1,0:T(8,128)(2,1)S(1)}, u32[]{:S(2)}, u32[]{:S(2)}) collective-permute-start(s16[32,80,128]{2,1,0:T(8,128)(2,1)S(1)} %all_to_all.16.own_ref), channel_id=1, source_target_pairs={{0,1},{1,0},{2,3},{3,2},{4,5},{5,4},{6,7},{7,6},{8,9},{9,8},{10,11... | collective-permute-start | bytes 1966088 | tf_op jit(solution)/shard_map/ppermute | solution.py:275
where the time goes:
time: 121 us; the launch traced here: 120 us
  blocking collectives  46.6 us (39%)
  Pallas kernels  41.6 us (34%)
  starting transfers between devices  18.3 us (15%)
  waiting for transfers between devices  6.8 us (6%)
  between operations  2.73 us (2%)
  local copies, waits for them, and re-layouts  2.12 us (2%)
  other arithmetic  2.11 us (2%)
    pallas_call x1, Pallas kernels, factor(): pl.pallas_call(factor_kernel, out_shape=jax.ShapeDtypeStruct(block_shape,...  37.2 us
    all_to_all x1, blocking collectives, per_device(): lax.all_to_all(both, 'param', split_axis=0, concat_axis=0, tiled=True)  24.7 us
    all_to_all x1, blocking collectives, per_device(): lax.all_to_all(jnp.broadcast_to(coded[None], (group,) + coded.shape), 'pa...  21.8 us
    all_to_all x1, starting transfers between devices, per_device(): lax.all_to_all(jnp.broadcast_to(feats[None], (chips,) + feats.shape), 'ex...  10 us
    ppermute x1, starting transfers between devices, per_device(): other = lax.ppermute(own, 'ex', [(i, i ^ 1) for i in range(ex_size)])  8.26 us
    all_to_all x1, waiting for transfers between devices, per_device(): lax.all_to_all(jnp.broadcast_to(feats[None], (chips,) + feats.shape), 'ex...  6.79 us
    pallas_call x1, Pallas kernels, project(): pl.pallas_call(functools.partial(project_kernel, seq_len, scale), out_sha...  4.38 us
  transfers between devices with their start and end apart: 2, of which 1 were waited for; matrix products, arithmetic and copies ran while one was open for 1% of the time, Pallas kernels for 0%

commit v1 on v0

--- a/solution.py
+++ b/solution.py
@@ -13,6 +13,7 @@
 DAMPING = 0.25
 PIECES = 3
 AHEAD = 4
+TOGETHER = 4
 LEVELS = 32767.0
 STEPS = 16.0
 f32, bf16 = jnp.float32, jnp.bfloat16
@@ -88,19 +89,30 @@
         if s == 0:
             small = {(k, l): entry(spread[SUB * q + l, q], k) for k in range(SUB) for l in range(k, SUB)}
             root = None
+        if s % TOGETHER == 0:
+            held = range(s, s + TOGETHER)
+            full = {k: entry(rows[q], k) for k in held}
+            across = {(k, c): entry(spread[c, q], k) for k in held for c in {c for c, _ in spread if c >= SUB * (q + 1)}}
         inverse = 1.0 / small[s, s]
         one_root = lax.rsqrt(small[s, s])
         root = one_root if root is None else jnp.where(sub == s, one_root, root)
         weights = {SUB * q + l: small[s, l] * inverse for l in range(s + 1, SUB)}
+        at_pivot, below = lane == i, sub > s
+        row = jnp.where(at_pivot, 1.0, full[s]) * inverse
+        later = [k for k in held if k > s]
+        for k in later:
+            full[k] = jnp.where(at_pivot, 0.0, full[k]) - small[s, k] * row
+        for c in sorted({c for c, _ in spread if c >= SUB * (q + 1)}):
+            value = across[s, c] if (s, c) in across else entry(spread[c, q], s)
+            weights[c] = value * inverse
+            for k in later:
+                if (k, c) in across:
+                    across[k, c] = across[k, c] - small[s, k] * weights[c]
         for l in range(s + 1, SUB):
             for m in range(l, SUB):
                 small[l, m] = small[l, m] - small[s, m] * weights[SUB * q + l]
-        at_pivot, below = lane == i, sub > s
-        row = jnp.where(at_pivot, 1.0, entry(rows[q], s)) * inverse
         own = jnp.where(below, spread[i, q], 0.0)
         for c in sorted({c for c, _ in spread if c > i}):
-            if c not in weights:
-                weights[c] = entry(spread[c, q], s) * inverse
             for p in range(q, groups):
                 if (c, p) in spread:
                     spread[c, p] = spread[c, p] - (own if p == q else spread[i, p]) * weights[c]
@@ -148,7 +160,7 @@
     return jnp.concatenate(parts, axis=0).astype(jnp.int16)
 
 
-def factor_kernel(place_ref, own_ref, other_ref, out_ref, lower, panels, feat, *pieces):
+def factor_kernel(place_ref, owners_ref, own_ref, other_ref, features_ref, out_ref, lower, panels, feat, *pieces):
     ft, lp = pieces[:PIECES], pieces[PIECES:]
     examples, nb, _ = feat.shape
     peers = own_ref.shape[0]
@@ -165,9 +177,16 @@
             return carry
 
         lax.fori_loop(0, peers, decode, 0)
+    height, width = out_ref.shape
+    ex, param = place_ref[0], place_ref[1]
+    mine = feat[owners_ref[0, param] * count + ex // 2]
     for b in range(nb):
+        features_ref[:, b * TILE : (b + 1) * TILE] = mine[b : b + 1]
+
+    def turn(b):
         for k, piece in enumerate(split(feat[:, b, :].T)):
             ft[k][b * TILE : (b + 1) * TILE, :] = piece
+
 
     def feats(lo, hi):
         return [ref[lo * TILE : hi * TILE, :] for ref in ft]
@@ -189,11 +208,14 @@
             block = block - times_t(lows(j, j + 1, known), lows(j, j + 1, known))
         return block
 
+    turn(0)
+    block, inverse = diagonal(0, 0), None
+    for b in range(1, nb):
+        turn(b)
     for i in range(nb):
         for c in range(i + 1, nb):
             lower[i * TILE : (i + 1) * TILE, c * TILE : (c + 1) * TILE] = jnp.zeros(shape, f32)
 
-    block, inverse = diagonal(0, 0), None
     for j in range(nb):
         if j >= 1 and j + 1 < nb:
             put(j + 1, nb, j - 1, times_t(split(panels[(j - 1) % 2, (j + 1) * TILE :, :]), inverse))
@@ -212,8 +234,6 @@
             first = split(first)
             block = ahead - times_t(first, first)
 
-    height, width = out_ref.shape
-    ex, param = place_ref[0], place_ref[1]
     per_tile = TILE // height
     taken = lower[pl.ds(pl.multiple_of(ex * width, width), width), pl.ds(pl.multiple_of(param // per_tile * TILE, TILE), TILE)]
     flipped = taken.T
@@ -223,20 +243,21 @@
     out_ref[...] = result
 
 
-def factor(place, own, other, examples, nb, block_shape):
+def factor(place, owners, own, other, examples, nb, block_shape):
     width = nb * TILE
+    smem = pl.BlockSpec(memory_space=pltpu.SMEM)
     vmem = pl.BlockSpec(memory_space=pltpu.VMEM)
     return pl.pallas_call(
         factor_kernel,
-        out_shape=jax.ShapeDtypeStruct(block_shape, f32),
-        in_specs=[pl.BlockSpec(memory_space=pltpu.SMEM), vmem, vmem],
-        out_specs=vmem,
+        out_shape=(jax.ShapeDtypeStruct((1, width), f32), jax.ShapeDtypeStruct(block_shape, f32)),
+        in_specs=[smem, smem, vmem, vmem],
+        out_specs=(vmem, vmem),
         scratch_shapes=[pltpu.VMEM((width, width), f32), pltpu.VMEM((2, width, TILE), f32), pltpu.VMEM((examples, nb, TILE), f32)]
         + [pltpu.VMEM((width, examples), bf16)] * PIECES
         + [pltpu.VMEM((width, width), bf16)] * PIECES,
         compiler_params=pltpu.CompilerParams(vmem_limit_bytes=48 * 2**20),
         name="factor",
-    )(place, own, other)
+    )(place, owners, own, other)
 
 
 def per_device(
@@ -274,14 +295,9 @@
     )
     other = lax.ppermute(own, "ex", [(i, i ^ 1) for i in range(ex_size)])
 
-    mine, at = owner_map[0, param], ex // 2
-    taken = lax.dynamic_slice(own, (mine, at * out_tiles, 0), (1, out_tiles, width)).astype(f32)
-    step = lax.dynamic_slice(own, (mine, chips * out_tiles + at, 0), (1, 1, width)).astype(f32)
-    features = (taken * (jnp.exp2(step / STEPS) / LEVELS)).reshape(1, out_tiles * width)
     block = (out_tiles * width // group, out_tiles * width // ex_size)
     place = jnp.stack([ex, param]).astype(jnp.int32)
-    r_block = factor(place, own, other, group * ex_size, out_tiles, block)
-    return features, r_block
+    return factor(place, owner_map, own, other, group * ex_size, out_tiles, block)
 
 
 def solution(mesh):

time: 121 us -> 120 us (level)
  between operations: 2.73 us -> 0.75 us
  waiting for transfers between devices: 6.8 us -> 8.4 us
    ppermute x1, waiting for transfers between devices: 0.01 us -> 1.61 us  [per_device(): other = lax.ppermute(own, 'ex', [(i, i ^ 1) for i in range(ex_size)])]
  transfers between devices with their start and end apart: 2 -> 2, of which waited for: 1 -> 2; matrix products, arithmetic and copies ran while one was open for 1% -> 0% of each run, Pallas kernels for 0% -> 0%
where the time goes in v1:
time: 120 us; the launch traced here: 119 us
  blocking collectives  46.6 us (39%)
  Pallas kernels  42.3 us (35%)
  starting transfers between devices  18.3 us (15%)
  waiting for transfers between devices  8.4 us (7%)
  local copies, waits for them, and re-layouts  1.53 us (1%)
  other arithmetic  1.49 us (1%)
    pallas_call x1, Pallas kernels, factor(): pl.pallas_call(factor_kernel, out_shape=(jax.ShapeDtypeStruct((1, width),...  38 us
    all_to_all x1, blocking collectives, per_device(): lax.all_to_all(both, 'param', split_axis=0, concat_axis=0, tiled=True)  24.7 us
    all_to_all x1, blocking collectives, per_device(): lax.all_to_all(jnp.broadcast_to(coded[None], (group,) + coded.shape), 'pa...  21.8 us
    all_to_all x1, starting transfers between devices, per_device(): lax.all_to_all(jnp.broadcast_to(feats[None], (chips,) + feats.shape), 'ex...  10 us
    ppermute x1, starting transfers between devices, per_device(): other = lax.ppermute(own, 'ex', [(i, i ^ 1) for i in range(ex_size)])  8.26 us
    all_to_all x1, waiting for transfers between devices, per_device(): lax.all_to_all(jnp.broadcast_to(feats[None], (chips,) + feats.shape), 'ex...  6.79 us
    pallas_call x1, Pallas kernels, project(): pl.pallas_call(functools.partial(project_kernel, seq_len, scale), out_sha...  4.38 us
  transfers between devices with their start and end apart: 2, of which 2 were waited for; matrix products, arithmetic and copies ran while one was open for 0% of the time, Pallas kernels for 0%

profile of v1, /device:TPU:1, one launch (start us, length us, event | category | flops | bytes accessed | tf_op | source)
XLA Modules:
  0.0 119.4 jit_solution(8649690578655031218)
XLA Ops:
  0.6 1.1 pad_maximum_fusion
  1.7 0.0 copy-start
  1.7 0.0 copy-start.2
  1.7 0.0 copy-start.3
  1.8 0.0 copy-start.4
  1.8 0.0 copy-start.5
  1.8 24.7 %all_to_all.15 = bf16[32,64,128]{2,1,0:T(8,128)(2,1)S(1)} all-to-all(bf16[32,64,128]{2,1,0:T(8,128)(2,1)S(1)} %pad_maximum_fusion), channel_id=1, replica_groups=mesh['param'=32,'ex'=16] {'param'}, dimensions={0} | all-to-all | bytes 1048576 | tf_op jit(solution)/shard_map/all_to_all | solution.py:273
  26.5 0.0 copy-start.1
  26.5 0.0 copy-done
  26.5 0.0 copy-done.2
  26.5 0.0 copy-done.3
  26.5 0.0 copy-done.4
  26.5 0.0 copy-done.5
  26.6 0.6 copy-done.1
  27.2 4.4 %project.1 = f32[8,128]{1,0:T(8,128)S(1)} custom-call(s32[256]{0:T(256)S(1)} %copy-done.1, s32[256]{0:T(256)S(1)} %copy-done.2, s32[256]{0:T(256)S(1)} %copy-done.3, s32[256]{0:T(256)S(1)} %copy-done.4, s32[256]{0:T(256)S(1)} %copy-done.5, bf16[2048,128]{1,0:T(8,128)(2,1)S(1)} %bitcast.7, bf16[16,128,128]{2,1,0:T(8,128)(2,1)S(1)} %copy-done), custom_call_target="tpu_custom_call" | custom-call | tf_op jit(solution)/shard_map/project/pallas_call | solution.py:53
  31.6 0.6 broadcast_in_dim.6
  32.2 10.0 %all-to-all-start.1 = ((f32[8,8,128]{2,1,0:T(8,128)}), f32[8,8,128]{2,1,0:T(8,128)S(1)}, u32[]{:S(2)}, u32[]{:S(2)}) async-start(f32[8,8,128]{2,1,0:T(8,128)} %broadcast_in_dim.6), calls=%async_computation.1 | async-start | bytes 65536 | tf_op jit(solution)/shard_map/all_to_all | solution.py:284
  42.2 0.1 pad.2.clone
  42.3 6.8 %all-to-all-done.1 = f32[8,8,128]{2,1,0:T(8,128)S(1)} async-done(((f32[8,8,128]{2,1,0:T(8,128)}), f32[8,8,128]{2,1,0:T(8,128)S(1)}, u32[]{:S(2)}, u32[]{:S(2)}) %all-to-all-start.1) | async-done | bytes 32800 | tf_op jit(solution)/shard_map/all_to_all | solution.py:284
  49.1 0.1 abs_reduce_fusion
  49.3 0.1 pad.1.clone
  49.4 0.1 fusion
  49.4 0.1 add_add_fusion
  49.5 0.1 broadcast_in_dim.8
  49.6 21.8 %all_to_all.16.own_ref = s16[32,80,128]{2,1,0:T(8,128)(2,1)S(1)} all-to-all(s16[32,80,128]{2,1,0:T(8,128)(2,1)S(1)} %broadcast_in_dim.8), channel_id=1, replica_groups=mesh['param'=32,'ex'=16] {'param'}, dimensions={0} | all-to-all | bytes 1310720 | tf_op jit(solution)/shard_map/all_to_all | solution.py:293
  71.4 8.3 %collective-permute-start = (s16[32,80,128]{2,1,0:T(8,128)(2,1)S(1)}, s16[32,80,128]{2,1,0:T(8,128)(2,1)S(1)}, u32[]{:S(2)}, u32[]{:S(2)}) collective-permute-start(s16[32,80,128]{2,1,0:T(8,128)(2,1)S(1)} %all_to_all.16.own_ref), channel_id=1, source_target_pairs={{0,1},{1,0},{2,3},{3,2},{4,5},{5,4},{6,7},{7,6},{8,9},{9,8},{10,11... | collective-permute-start | bytes 1966088 | tf_op jit(solution)/shard_map/ppermute | solution.py:296
  79.7 0.0 copy-start.6
  79.7 0.1 pad_add_fusion.place_ref
  79.8 1.6 %collective-permute-done.other_ref = s16[32,80,128]{2,1,0:T(8,128)(2,1)S(1)} collective-permute-done((s16[32,80,128]{2,1,0:T(8,128)(2,1)S(1)}, s16[32,80,128]{2,1,0:T(8,128)(2,1)S(1)}, u32[]{:S(2)}, u32[]{:S(2)}) %collective-permute-start) | collective-permute-done | bytes 655392 | tf_op jit(solution)/shard_map/ppermute | solution.py:296
  81.4 0.0 copy-done.6
  81.4 38.0 %factor.1 = (f32[1,1024]{1,0:T(1,128)}, f32[32,64]{1,0:T(8,128)}) custom-call(s32[2]{0:T(128)S(1)} %pad_add_fusion.place_ref, s32[1,32]{1,0:T(1,128)S(1)} %copy-done.6, s16[32,80,128]{2,1,0:T(8,128)(2,1)S(1)} %all_to_all.16.own_ref, s16[32,80,128]{2,1,0:T(8,128)(2,1)S(1)} %collective-permute-done.other_ref), custom_call_target="tpu_custom_call" | custom-call | tf_op jit(solution)/shard_map/factor/pallas_call | solution.py:250
  (2 shorter events, 0.0 us)
Async XLA Ops:
  1.7 24.8 %copy-start = (bf16[16,128,128]{2,1,0:T(8,128)(2,1)S(1)}, bf16[16,128,128]{2,1,0:T(8,128)(2,1)}, u32[]{:S(2)}) copy-start(bf16[16,128,128]{2,1,0:T(8,128)(2,1)} %bank_ref.1) | copy-start | bytes 1572868
  1.7 24.8 %copy-start.2 = (s32[256]{0:T(256)S(1)}, s32[256]{0:T(256)}, u32[]{:S(2)}) copy-start(s32[256]{0:T(256)} %cols_ref.1) | copy-start | bytes 3076
  1.7 24.8 %copy-start.3 = (s32[256]{0:T(256)S(1)}, s32[256]{0:T(256)}, u32[]{:S(2)}) copy-start(s32[256]{0:T(256)} %outs_ref.1) | copy-start | bytes 3076
  1.8 24.8 %copy-start.4 = (s32[256]{0:T(256)S(1)}, s32[256]{0:T(256)}, u32[]{:S(2)}) copy-start(s32[256]{0:T(256)} %lefts_ref.1) | copy-start | bytes 3076
  1.8 24.8 %copy-start.5 = (s32[256]{0:T(256)S(1)}, s32[256]{0:T(256)}, u32[]{:S(2)}) copy-start(s32[256]{0:T(256)} %rights_ref.1) | copy-start | bytes 3076
  26.5 0.7 copy-start.1
  32.2 16.9 %all-to-all-start.1 = ((f32[8,8,128]{2,1,0:T(8,128)}), f32[8,8,128]{2,1,0:T(8,128)S(1)}, u32[]{:S(2)}, u32[]{:S(2)}) async-start(f32[8,8,128]{2,1,0:T(8,128)} %broadcast_in_dim.6), calls=%async_computation.1 | async-start | bytes 65536 | tf_op jit(solution)/shard_map/all_to_all | solution.py:284
  71.4 10.0 %collective-permute-start = (s16[32,80,128]{2,1,0:T(8,128)(2,1)S(1)}, s16[32,80,128]{2,1,0:T(8,128)(2,1)S(1)}, u32[]{:S(2)}, u32[]{:S(2)}) collective-permute-start(s16[32,80,128]{2,1,0:T(8,128)(2,1)S(1)} %all_to_all.16.own_ref), channel_id=1, source_target_pairs={{0,1},{1,0},{2,3},{3,2},{4,5},{5,4},{6,7},{7,6},{8,9},{9,8},{10,11... | collective-permute-start | bytes 1966088 | tf_op jit(solution)/shard_map/ppermute | solution.py:296
  79.7 1.7 %copy-start.6 = (s32[1,32]{1,0:T(1,128)S(1)}, s32[1,32]{1,0:T(1,128)}, u32[]{:S(2)}) copy-start(s32[1,32]{1,0:T(1,128)} %owners_ref.1) | copy-start | bytes 388

commit v2 on v1

--- a/solution.py
+++ b/solution.py
@@ -12,8 +12,8 @@
 SUB = 8
 DAMPING = 0.25
 PIECES = 3
-AHEAD = 4
-TOGETHER = 4
+AHEAD = 5
+DEEP = 10
 LEVELS = 32767.0
 STEPS = 16.0
 f32, bf16 = jnp.float32, jnp.bfloat16
@@ -43,16 +43,16 @@
         return carry
 
     lax.fori_loop(0, rows_ref.shape[0] // unroll, add_slots, 0)
-    feat_ref[...] = jnp.sum(acc[...], axis=1) * scale
-
-
-def project(x, bank, ids, seq_len, out_tiles):
+    feat_ref[...] = jnp.broadcast_to((jnp.sum(acc[...], axis=1) * scale)[None], feat_ref.shape)
+
+
+def project(x, bank, ids, seq_len, out_tiles, copies):
     scale = 1.0 / math.sqrt(seq_len * ids[0].shape[0] / out_tiles)
     smem = pl.BlockSpec(memory_space=pltpu.SMEM)
     vmem = pl.BlockSpec(memory_space=pltpu.VMEM)
     return pl.pallas_call(
         functools.partial(project_kernel, seq_len, scale),
-        out_shape=jax.ShapeDtypeStruct((out_tiles, TILE), f32),
+        out_shape=jax.ShapeDtypeStruct((copies, out_tiles, TILE), f32),
         in_specs=[smem] * 5 + [vmem] * 2,
         out_specs=vmem,
         scratch_shapes=[
@@ -77,45 +77,26 @@
         return jnp.broadcast_to(x[s : s + 1, :], (SUB, TILE))
 
     def wanted(i, first):
-        for c in range(max(i, 0), min(TILE, i + SUB + 1)):
+        for c in range(max(i, 0), min(TILE, i + DEEP + 1)):
             for p in range(first, groups):
                 if c <= i + AHEAD or p <= c // SUB:
                     yield c, p
 
     spread = {(c, p): column(p, c) for c, p in wanted(-1, 0)}
-    small, upper, inverse_lower = {}, [], []
+    upper, inverse_lower = [], []
     for i in range(TILE):
         q, s = divmod(i, SUB)
-        if s == 0:
-            small = {(k, l): entry(spread[SUB * q + l, q], k) for k in range(SUB) for l in range(k, SUB)}
-            root = None
-        if s % TOGETHER == 0:
-            held = range(s, s + TOGETHER)
-            full = {k: entry(rows[q], k) for k in held}
-            across = {(k, c): entry(spread[c, q], k) for k in held for c in {c for c, _ in spread if c >= SUB * (q + 1)}}
-        inverse = 1.0 / small[s, s]
-        one_root = lax.rsqrt(small[s, s])
-        root = one_root if root is None else jnp.where(sub == s, one_root, root)
-        weights = {SUB * q + l: small[s, l] * inverse for l in range(s + 1, SUB)}
+        pivot = entry(spread[i, q], s)
+        inverse, one_root = 1.0 / pivot, lax.rsqrt(pivot)
+        root = one_root if s == 0 else jnp.where(sub == s, one_root, root)
         at_pivot, below = lane == i, sub > s
-        row = jnp.where(at_pivot, 1.0, full[s]) * inverse
-        later = [k for k in held if k > s]
-        for k in later:
-            full[k] = jnp.where(at_pivot, 0.0, full[k]) - small[s, k] * row
-        for c in sorted({c for c, _ in spread if c >= SUB * (q + 1)}):
-            value = across[s, c] if (s, c) in across else entry(spread[c, q], s)
-            weights[c] = value * inverse
-            for k in later:
-                if (k, c) in across:
-                    across[k, c] = across[k, c] - small[s, k] * weights[c]
-        for l in range(s + 1, SUB):
-            for m in range(l, SUB):
-                small[l, m] = small[l, m] - small[s, m] * weights[SUB * q + l]
+        row = jnp.where(at_pivot, 1.0, entry(rows[q], s)) * inverse
         own = jnp.where(below, spread[i, q], 0.0)
         for c in sorted({c for c, _ in spread if c > i}):
-            for p in range(q, groups):
+            weight = entry(spread[c, q], s) * inverse
+            for p in range(q if s < SUB - 1 else q + 1, groups):
                 if (c, p) in spread:
-                    spread[c, p] = spread[c, p] - (own if p == q else spread[i, p]) * weights[c]
+                    spread[c, p] = spread[c, p] - (own if p == q else spread[i, p]) * weight
         if s < SUB - 1:
             rows[q] = jnp.where(at_pivot & below, 0.0, rows[q]) - own * row
         for p in range(q + 1, groups):
@@ -156,7 +137,7 @@
     step = jnp.ceil(STEPS * jnp.log2(jnp.maximum(top, 1e-30)))
     coded = jnp.clip(jnp.round(rows * (LEVELS * jnp.exp2(step / -STEPS))), -LEVELS, LEVELS)
     scales = jnp.broadcast_to(step[:, 0], (count, width))
-    parts = [coded.reshape(count * blocks, width), scales, jnp.zeros((-count % 16, width), f32)]
+    parts = [coded.reshape(count * blocks, width), scales, jnp.zeros((-count % SUB, width), f32)]
     return jnp.concatenate(parts, axis=0).astype(jnp.int16)
 
 
@@ -176,7 +157,7 @@
             feat[pl.ds(h * peers * count + peer * count, count)] = values
             return carry
 
-        lax.fori_loop(0, peers, decode, 0)
+        lax.fori_loop(0, peers, decode, 0, unroll=4)
     height, width = out_ref.shape
     ex, param = place_ref[0], place_ref[1]
     mine = feat[owners_ref[0, param] * count + ex // 2]
@@ -277,12 +258,13 @@
         (tile_rows, tile_cols, tile_out, bank_left, bank_right),
         seq_len,
         out_tiles,
+        ex_size // 2,
     )
 
     chips = ex_size // 2
     lines = [[2 * z + core for z in range(chips)] for core in range(2)]
     line = lax.all_to_all(
-        jnp.broadcast_to(feats[None], (chips,) + feats.shape),
+        feats,
         "ex",
         split_axis=0,
         concat_axis=0,

time: 120 us -> 115 us (0.958)
  blocking collectives: 46.6 us -> 61.9 us
  starting transfers between devices: 18.3 us -> 8.16 us
  waiting for transfers between devices: 8.4 us -> 1.52 us
  Pallas kernels: 42.3 us -> 40.1 us
    all_to_all x0 -> x1, blocking collectives: none -> 16.7 us  [per_device(): lax.all_to_all(feats, 'ex', split_axis=0, concat_axis=0, axis_index_group...]
    all_to_all x1 -> x0, starting transfers between devices: 10 us -> none  [per_device(): lax.all_to_all(jnp.broadcast_to(feats[None], (chips,) + feats.shape), 'ex...]
    all_to_all x1 -> x0, waiting for transfers between devices: 6.79 us -> none  [per_device(): lax.all_to_all(jnp.broadcast_to(feats[None], (chips,) + feats.shape), 'ex...]
    pallas_call x1, Pallas kernels: 38 us -> 35.7 us  [factor(): pl.pallas_call(factor_kernel, out_shape=(jax.ShapeDtypeStruct((1, width),...]
    all_to_all x1, blocking collectives: 21.8 us -> 20.4 us  [per_device(): lax.all_to_all(jnp.broadcast_to(coded[None], (group,) + coded.shape), 'pa...]
  transfers between devices with their start and end apart: 2 -> 1, of which waited for: 2 -> 1; matrix products, arithmetic and copies ran while one was open for 0% -> 0% of each run, Pallas kernels for 0% -> 0%
where the time goes in v2:
time: 115 us
  blocking collectives  61.9 us (54%)
  Pallas kernels  40.1 us (35%)
  starting transfers between devices  8.16 us (7%)
  waiting for transfers between devices  1.52 us (1%)
  other arithmetic  1.47 us (1%)
    pallas_call x1, Pallas kernels, factor(): pl.pallas_call(factor_kernel, out_shape=(jax.ShapeDtypeStruct((1, width),...  35.7 us
    all_to_all x1, blocking collectives, per_device(): lax.all_to_all(both, 'param', split_axis=0, concat_axis=0, tiled=True)  24.7 us
    all_to_all x1, blocking collectives, per_device(): lax.all_to_all(jnp.broadcast_to(coded[None], (group,) + coded.shape), 'pa...  20.4 us
    all_to_all x1, blocking collectives, per_device(): lax.all_to_all(feats, 'ex', split_axis=0, concat_axis=0, axis_index_group...  16.7 us
    ppermute x1, starting transfers between devices, per_device(): other = lax.ppermute(own, 'ex', [(i, i ^ 1) for i in range(ex_size)])  8.16 us
    pallas_call x1, Pallas kernels, project(): pl.pallas_call(functools.partial(project_kernel, seq_len, scale), out_sha...  4.38 us
  transfers between devices with their start and end apart: 1, of which 1 were waited for; matrix products, arithmetic and copies ran while one was open for 0% of the time, Pallas kernels for 0%

profile of v2, /device:TPU:1, one launch (start us, length us, event | category | flops | bytes accessed | tf_op | source)
XLA Modules:
  0.0 114.7 jit_solution(14119858409602176191)
XLA Ops:
  0.6 1.1 pad_maximum_fusion
  1.7 0.0 copy-start
  1.7 0.0 copy-start.2
  1.7 0.0 copy-start.3
  1.8 0.0 copy-start.4
  1.8 0.0 copy-start.5
  1.8 24.7 %all_to_all.15 = bf16[32,64,128]{2,1,0:T(8,128)(2,1)S(1)} all-to-all(bf16[32,64,128]{2,1,0:T(8,128)(2,1)S(1)} %pad_maximum_fusion), channel_id=1, replica_groups=mesh['param'=32,'ex'=16] {'param'}, dimensions={0} | all-to-all | bytes 1048576 | tf_op jit(solution)/shard_map/all_to_all | solution.py:254
  26.5 0.0 copy-start.1
  26.5 0.0 copy-done
  26.5 0.0 copy-done.2
  26.5 0.0 copy-done.3
  26.5 0.0 copy-done.4
  26.5 0.0 copy-done.5
  26.6 0.6 copy-done.1
  27.2 4.4 %project.1 = f32[8,8,128]{2,1,0:T(8,128)S(1)} custom-call(s32[256]{0:T(256)S(1)} %copy-done.1, s32[256]{0:T(256)S(1)} %copy-done.2, s32[256]{0:T(256)S(1)} %copy-done.3, s32[256]{0:T(256)S(1)} %copy-done.4, s32[256]{0:T(256)S(1)} %copy-done.5, bf16[2048,128]{1,0:T(8,128)(2,1)S(1)} %bitcast.7, bf16[16,128,128]{2,1,0:T(8,128)(2,1)S(1)} %copy-done), custom_call_target="tpu_custom_call" | custom-call | tf_op jit(solution)/shard_map/project/pallas_call | solution.py:53
  31.6 16.7 %all_to_all.16 = f32[8,8,128]{2,1,0:T(8,128)S(1)} all-to-all(f32[8,8,128]{2,1,0:T(8,128)S(1)} %project.1), channel_id=1, replica_groups={{0,2,4,6,8,10,12,14},{1,3,5,7,9,11,13,15},{16,18,20,22,24,26,28,30},{17..., dimensions={0} | all-to-all | bytes 65536 | tf_op jit(solution)/shard_map/all_to_all | solution.py:266
  48.3 0.1 abs_reduce_fusion
  48.5 0.1 pad.1.clone
  48.5 0.1 fusion
  48.6 0.1 pad_add_fusion
  48.7 0.1 broadcast_in_dim.2
  48.8 20.4 %all_to_all.17.own_ref = s16[32,72,128]{2,1,0:T(8,128)(2,1)S(1)} all-to-all(s16[32,72,128]{2,1,0:T(8,128)(2,1)S(1)} %broadcast_in_dim.2), channel_id=1, replica_groups=mesh['param'=32,'ex'=16] {'param'}, dimensions={0} | all-to-all | bytes 1179648 | tf_op jit(solution)/shard_map/all_to_all | solution.py:275
  69.2 8.2 %collective-permute-start = (s16[32,72,128]{2,1,0:T(8,128)(2,1)S(1)}, s16[32,72,128]{2,1,0:T(8,128)(2,1)S(1)}, u32[]{:S(2)}, u32[]{:S(2)}) collective-permute-start(s16[32,72,128]{2,1,0:T(8,128)(2,1)S(1)} %all_to_all.17.own_ref), channel_id=1, source_target_pairs={{0,1},{1,0},{2,3},{3,2},{4,5},{5,4},{6,7},{7,6},{8,9},{9,8},{10,11... | collective-permute-start | bytes 1769480 | tf_op jit(solution)/shard_map/ppermute | solution.py:278
  77.4 0.0 copy-start.6
  77.4 0.1 pad_add_fusion.1.place_ref
  77.5 1.5 %collective-permute-done.other_ref = s16[32,72,128]{2,1,0:T(8,128)(2,1)S(1)} collective-permute-done((s16[32,72,128]{2,1,0:T(8,128)(2,1)S(1)}, s16[32,72,128]{2,1,0:T(8,128)(2,1)S(1)}, u32[]{:S(2)}, u32[]{:S(2)}) %collective-permute-start) | collective-permute-done | bytes 589856 | tf_op jit(solution)/shard_map/ppermute | solution.py:278
  79.0 0.0 copy-done.6
  79.0 35.7 %factor.1 = (f32[1,1024]{1,0:T(1,128)}, f32[32,64]{1,0:T(8,128)}) custom-call(s32[2]{0:T(128)S(1)} %pad_add_fusion.1.place_ref, s32[1,32]{1,0:T(1,128)S(1)} %copy-done.6, s16[32,72,128]{2,1,0:T(8,128)(2,1)S(1)} %all_to_all.17.own_ref, s16[32,72,128]{2,1,0:T(8,128)(2,1)S(1)} %collective-permute-done.other_ref), custom_call_target="tpu_custom_call" | custom-call | tf_op jit(solution)/shard_map/factor/pallas_call | solution.py:231
  (1 shorter events, 0.0 us)
Async XLA Ops:
  1.7 24.8 %copy-start = (bf16[16,128,128]{2,1,0:T(8,128)(2,1)S(1)}, bf16[16,128,128]{2,1,0:T(8,128)(2,1)}, u32[]{:S(2)}) copy-start(bf16[16,128,128]{2,1,0:T(8,128)(2,1)} %bank_ref.1) | copy-start | bytes 1572868
  1.7 24.8 %copy-start.2 = (s32[256]{0:T(256)S(1)}, s32[256]{0:T(256)}, u32[]{:S(2)}) copy-start(s32[256]{0:T(256)} %cols_ref.1) | copy-start | bytes 3076
  1.7 24.8 %copy-start.3 = (s32[256]{0:T(256)S(1)}, s32[256]{0:T(256)}, u32[]{:S(2)}) copy-start(s32[256]{0:T(256)} %outs_ref.1) | copy-start | bytes 3076
  1.8 24.8 %copy-start.4 = (s32[256]{0:T(256)S(1)}, s32[256]{0:T(256)}, u32[]{:S(2)}) copy-start(s32[256]{0:T(256)} %lefts_ref.1) | copy-start | bytes 3076
  1.8 24.8 %copy-start.5 = (s32[256]{0:T(256)S(1)}, s32[256]{0:T(256)}, u32[]{:S(2)}) copy-start(s32[256]{0:T(256)} %rights_ref.1) | copy-start | bytes 3076
  26.5 0.7 copy-start.1
  69.2 9.8 %collective-permute-start = (s16[32,72,128]{2,1,0:T(8,128)(2,1)S(1)}, s16[32,72,128]{2,1,0:T(8,128)(2,1)S(1)}, u32[]{:S(2)}, u32[]{:S(2)}) collective-permute-start(s16[32,72,128]{2,1,0:T(8,128)(2,1)S(1)} %all_to_all.17.own_ref), channel_id=1, source_target_pairs={{0,1},{1,0},{2,3},{3,2},{4,5},{5,4},{6,7},{7,6},{8,9},{9,8},{10,11... | collective-permute-start | bytes 1769480 | tf_op jit(solution)/shard_map/ppermute | solution.py:278
  77.4 1.6 %copy-start.6 = (s32[1,32]{1,0:T(1,128)S(1)}, s32[1,32]{1,0:T(1,128)}, u32[]{:S(2)}) copy-start(s32[1,32]{1,0:T(1,128)} %owners_ref.1) | copy-start | bytes 388

commit v3 on v2

--- a/solution.py
+++ b/solution.py
@@ -20,8 +20,16 @@
 
 
 def project_kernel(
-    seq_len, scale, rows_ref, cols_ref, outs_ref, lefts_ref, rights_ref, x_ref, bank_ref, feat_ref, table, acc
+    seq_len, scale, rows_in, cols_in, outs_in, lefts_in, rights_in, x_ref, bank_ref, feat_ref, table, acc, *held
 ):
+    lists, arrived = held[:-1], held[-1]
+    copies = [
+        pltpu.make_async_copy(source, target, arrived.at[k])
+        for k, (source, target) in enumerate(zip((rows_in, cols_in, outs_in, lefts_in, rights_in), lists))
+    ]
+    for copy in copies:
+        copy.start()
+    rows_ref, cols_ref, outs_ref, lefts_ref, rights_ref = lists
     banks = bank_ref.shape[0]
     for pair in range(banks // 2):
         tiles = jnp.concatenate([bank_ref[2 * pair], bank_ref[2 * pair + 1]], axis=1)
@@ -29,6 +37,8 @@
         table[2 * pair] = both[:, :TILE]
         table[2 * pair + 1] = both[:, TILE:]
     acc[...] = jnp.zeros_like(acc)
+    for copy in copies:
+        copy.wait()
     unroll = 8
 
     def add_slots(group, carry):
@@ -48,17 +58,19 @@
 
 def project(x, bank, ids, seq_len, out_tiles, copies):
     scale = 1.0 / math.sqrt(seq_len * ids[0].shape[0] / out_tiles)
-    smem = pl.BlockSpec(memory_space=pltpu.SMEM)
+    left = pl.BlockSpec(memory_space=pl.ANY)
     vmem = pl.BlockSpec(memory_space=pltpu.VMEM)
     return pl.pallas_call(
         functools.partial(project_kernel, seq_len, scale),
         out_shape=jax.ShapeDtypeStruct((copies, out_tiles, TILE), f32),
-        in_specs=[smem] * 5 + [vmem] * 2,
+        in_specs=[left] * 5 + [vmem] * 2,
         out_specs=vmem,
         scratch_shapes=[
             pltpu.VMEM((bank.shape[0], x.shape[0], TILE), f32),
             pltpu.VMEM((out_tiles, SUB, TILE), f32),
-        ],
+        ]
+        + [pltpu.SMEM(ids[0].shape, jnp.int32)] * 5
+        + [pltpu.SemaphoreType.DMA((5,))],
         compiler_params=pltpu.CompilerParams(vmem_limit_bytes=40 * 2**20),
         name="project",
     )(*ids, x, bank)
@@ -157,7 +169,7 @@
             feat[pl.ds(h * peers * count + peer * count, count)] = values
             return carry
 
-        lax.fori_loop(0, peers, decode, 0, unroll=4)
+        lax.fori_loop(0, peers, decode, 0, unroll=8)
     height, width = out_ref.shape
     ex, param = place_ref[0], place_ref[1]
     mine = feat[owners_ref[0, param] * count + ex // 2]

time: 115 us -> 114 us (level)
  no operation moved by 1% of the time
where the time goes in v3:
time: 114 us
  blocking collectives  61.9 us (54%)
  Pallas kernels  39.5 us (35%)
  starting transfers between devices  8.13 us (7%)
  waiting for transfers between devices  1.52 us (1%)
  other arithmetic  1.47 us (1%)
    pallas_call x1, Pallas kernels, factor(): pl.pallas_call(factor_kernel, out_shape=(jax.ShapeDtypeStruct((1, width),...  35.6 us
    all_to_all x1, blocking collectives, per_device(): lax.all_to_all(both, 'param', split_axis=0, concat_axis=0, tiled=True)  24.7 us
    all_to_all x1, blocking collectives, per_device(): lax.all_to_all(jnp.broadcast_to(coded[None], (group,) + coded.shape), 'pa...  20.4 us
    all_to_all x1, blocking collectives, per_device(): lax.all_to_all(feats, 'ex', split_axis=0, concat_axis=0, axis_index_group...  16.7 us
    ppermute x1, starting transfers between devices, per_device(): other = lax.ppermute(own, 'ex', [(i, i ^ 1) for i in range(ex_size)])  8.13 us
    pallas_call x1, Pallas kernels, project(): pl.pallas_call(functools.partial(project_kernel, seq_len, scale), out_sha...  3.86 us
  transfers between devices with their start and end apart: 1, of which 1 were waited for; matrix products, arithmetic and copies ran while one was open for 0% of the time, Pallas kernels for 0%

profile of v3, /device:TPU:1, one launch (start us, length us, event | category | flops | bytes accessed | tf_op | source)
XLA Modules:
  0.0 114.1 jit_solution(2158808147873189858)
XLA Ops:
  0.6 1.1 pad_maximum_fusion
  1.7 0.0 copy-start
  1.7 0.0 copy-start.2
  1.7 0.0 copy-start.3
  1.8 0.0 copy-start.4
  1.8 0.0 copy-start.5
  1.8 24.7 %all_to_all.15 = bf16[32,64,128]{2,1,0:T(8,128)(2,1)S(1)} all-to-all(bf16[32,64,128]{2,1,0:T(8,128)(2,1)S(1)} %pad_maximum_fusion), channel_id=1, replica_groups=mesh['param'=32,'ex'=16] {'param'}, dimensions={0} | all-to-all | bytes 1048576 | tf_op jit(solution)/shard_map/all_to_all | solution.py:266
  26.5 0.0 copy-start.1
  26.5 0.0 copy-done
  26.5 0.0 copy-done.2
  26.5 0.0 copy-done.3
  26.5 0.0 copy-done.4
  26.5 0.0 copy-done.5
  26.6 0.6 copy-done.1
  27.2 3.9 %project.1 = f32[8,8,128]{2,1,0:T(8,128)S(1)} custom-call(s32[256]{0:T(256)S(1)} %copy-done.1, s32[256]{0:T(256)S(1)} %copy-done.2, s32[256]{0:T(256)S(1)} %copy-done.3, s32[256]{0:T(256)S(1)} %copy-done.4, s32[256]{0:T(256)S(1)} %copy-done.5, bf16[2048,128]{1,0:T(8,128)(2,1)S(1)} %bitcast.7, bf16[16,128,128]{2,1,0:T(8,128)(2,1)S(1)} %copy-done), custom_call_target="tpu_custom_call" | custom-call | tf_op jit(solution)/shard_map/project/pallas_call | solution.py:63
  31.1 16.7 %all_to_all.16 = f32[8,8,128]{2,1,0:T(8,128)S(1)} all-to-all(f32[8,8,128]{2,1,0:T(8,128)S(1)} %project.1), channel_id=1, replica_groups={{0,2,4,6,8,10,12,14},{1,3,5,7,9,11,13,15},{16,18,20,22,24,26,28,30},{17..., dimensions={0} | all-to-all | bytes 65536 | tf_op jit(solution)/shard_map/all_to_all | solution.py:278
  47.8 0.1 abs_reduce_fusion
  48.0 0.1 pad.1.clone
  48.0 0.1 fusion
  48.1 0.1 pad_add_fusion
  48.2 0.1 broadcast_in_dim.2
  48.3 20.4 %all_to_all.17.own_ref = s16[32,72,128]{2,1,0:T(8,128)(2,1)S(1)} all-to-all(s16[32,72,128]{2,1,0:T(8,128)(2,1)S(1)} %broadcast_in_dim.2), channel_id=1, replica_groups=mesh['param'=32,'ex'=16] {'param'}, dimensions={0} | all-to-all | bytes 1179648 | tf_op jit(solution)/shard_map/all_to_all | solution.py:287
  68.7 8.1 %collective-permute-start = (s16[32,72,128]{2,1,0:T(8,128)(2,1)S(1)}, s16[32,72,128]{2,1,0:T(8,128)(2,1)S(1)}, u32[]{:S(2)}, u32[]{:S(2)}) collective-permute-start(s16[32,72,128]{2,1,0:T(8,128)(2,1)S(1)} %all_to_all.17.own_ref), channel_id=1, source_target_pairs={{0,1},{1,0},{2,3},{3,2},{4,5},{5,4},{6,7},{7,6},{8,9},{9,8},{10,11... | collective-permute-start | bytes 1769480 | tf_op jit(solution)/shard_map/ppermute | solution.py:290
  76.9 0.0 copy-start.6
  76.9 0.1 pad_add_fusion.1.place_ref
  77.0 1.5 %collective-permute-done.other_ref = s16[32,72,128]{2,1,0:T(8,128)(2,1)S(1)} collective-permute-done((s16[32,72,128]{2,1,0:T(8,128)(2,1)S(1)}, s16[32,72,128]{2,1,0:T(8,128)(2,1)S(1)}, u32[]{:S(2)}, u32[]{:S(2)}) %collective-permute-start) | collective-permute-done | bytes 589856 | tf_op jit(solution)/shard_map/ppermute | solution.py:290
  78.5 0.0 copy-done.6
  78.5 35.6 %factor.1 = (f32[1,1024]{1,0:T(1,128)}, f32[32,64]{1,0:T(8,128)}) custom-call(s32[2]{0:T(128)S(1)} %pad_add_fusion.1.place_ref, s32[1,32]{1,0:T(1,128)S(1)} %copy-done.6, s16[32,72,128]{2,1,0:T(8,128)(2,1)S(1)} %all_to_all.17.own_ref, s16[32,72,128]{2,1,0:T(8,128)(2,1)S(1)} %collective-permute-done.other_ref), custom_call_target="tpu_custom_call" | custom-call | tf_op jit(solution)/shard_map/factor/pallas_call | solution.py:243
  (1 shorter events, 0.0 us)
Async XLA Ops:
  1.7 24.8 %copy-start = (bf16[16,128,128]{2,1,0:T(8,128)(2,1)S(1)}, bf16[16,128,128]{2,1,0:T(8,128)(2,1)}, u32[]{:S(2)}) copy-start(bf16[16,128,128]{2,1,0:T(8,128)(2,1)} %bank_ref.1) | copy-start | bytes 1572868
  1.7 24.8 %copy-start.2 = (s32[256]{0:T(256)S(1)}, s32[256]{0:T(256)}, u32[]{:S(2)}) copy-start(s32[256]{0:T(256)} %cols_in.1) | copy-start | bytes 3076
  1.7 24.8 %copy-start.3 = (s32[256]{0:T(256)S(1)}, s32[256]{0:T(256)}, u32[]{:S(2)}) copy-start(s32[256]{0:T(256)} %outs_in.1) | copy-start | bytes 3076
  1.8 24.8 %copy-start.4 = (s32[256]{0:T(256)S(1)}, s32[256]{0:T(256)}, u32[]{:S(2)}) copy-start(s32[256]{0:T(256)} %lefts_in.1) | copy-start | bytes 3076
  1.8 24.8 %copy-start.5 = (s32[256]{0:T(256)S(1)}, s32[256]{0:T(256)}, u32[]{:S(2)}) copy-start(s32[256]{0:T(256)} %rights_in.1) | copy-start | bytes 3076
  26.5 0.7 copy-start.1
  68.7 9.7 %collective-permute-start = (s16[32,72,128]{2,1,0:T(8,128)(2,1)S(1)}, s16[32,72,128]{2,1,0:T(8,128)(2,1)S(1)}, u32[]{:S(2)}, u32[]{:S(2)}) collective-permute-start(s16[32,72,128]{2,1,0:T(8,128)(2,1)S(1)} %all_to_all.17.own_ref), channel_id=1, source_target_pairs={{0,1},{1,0},{2,3},{3,2},{4,5},{5,4},{6,7},{7,6},{8,9},{9,8},{10,11... | collective-permute-start | bytes 1769480 | tf_op jit(solution)/shard_map/ppermute | solution.py:290
  76.9 1.6 %copy-start.6 = (s32[1,32]{1,0:T(1,128)S(1)}, s32[1,32]{1,0:T(1,128)}, u32[]{:S(2)}) copy-start(s32[1,32]{1,0:T(1,128)} %owners_ref.1) | copy-start | bytes 388
